TPU v7x, 32 devices: a whole 2x2x4 slice. The times are simulated.
32 devices in a mesh: wide: 8 (over z, y), narrow: 4 (over x, core).
Axes of the slice: x: 2, y: 2, z: 4, core: 2. Of those that a mesh axis runs over, the one named last changes fastest.
Arguments:
- gradients: bfloat16 [32, 16, 1024], P(None, 'narrow', 'wide'), may hold values from -4000 to 4000
- offsets: int32 [16], P('narrow'), may hold values from 0 to 1048575
- seeds: int32 [2, 4096], replicated, may hold values from 1 to 8190
- inv_kernel: float32 [4096, 4096], P('wide', 'narrow'), may hold values from -2 to 2
- sketches: float32 [1024, 4096], P('wide', 'narrow'), may hold values from -6 to 6
Outputs:
- scores: float32 [32, 1024], P('narrow', 'wide')
All inputs are finite; a program needn't handle non-finite values.
Results may differ from a plain program's by a relative error of at most 0.0023.
Values sent between devices are 32-bit elements; how exact they have to be, the bound alone decides.
A program may use at most 64 MiB of HBM per device.

v0:
```python
import functools
import math

import jax
import jax.numpy as jnp
from jax import lax
from jax.experimental import pallas as pl
from jax.experimental.pallas import tpu as pltpu
from jax.sharding import PartitionSpec as P

modulus = 8191
turn = 2.0 * math.pi / 8191.0
epsilon = 1e-06


def cosine_block(param_index, mults, adds):
    phase = (
        (param_index % modulus)[:, None] * (mults % modulus)[None, :] + adds[None, :]
    ) % modulus
    return jnp.cos(phase.astype(jnp.float32) * turn).astype(jnp.bfloat16)


def body(gradients, offsets, seeds, inv_kernel, sketches):
    queries = gradients.shape[0]
    cols_dev = gradients.shape[2]
    flat_grad = gradients.reshape(queries, -1)
    width = seeds.shape[1]
    n_wide = lax.axis_size("wide")
    n_narrow = lax.axis_size("narrow")
    param_index = (
        offsets[:, None]
        + lax.axis_index("wide") * cols_dev
        + jnp.arange(cols_dev, dtype=jnp.int32)[None, :]
    ).reshape(-1)
    local_squares = jnp.sum(jnp.square(flat_grad.astype(jnp.float32)), axis=1)
    start = jnp.int32(0)
    step = min(lax.axis_size("wide") * (width // n_wide), 512)
    pieces = []
    for block_id in range(lax.axis_size("wide") * (width // n_wide) // step):
        begin = start + block_id * step
        mults = lax.dynamic_slice_in_dim(seeds[0], begin, step)
        adds = lax.dynamic_slice_in_dim(seeds[1], begin, step)
        table = cosine_block(param_index, mults, adds)
        term = jnp.einsum("pk,qp->kq", table, flat_grad, preferred_element_type=jnp.float32)
        pieces.append(term)
    owned = lax.psum_scatter(
        jnp.concatenate(pieces, axis=0), "wide", scatter_dimension=0, tiled=True
    )
    owned = lax.psum(owned, "narrow")
    kernel_part = lax.dot_general(
        owned,
        inv_kernel,
        (((0,), (0,)), ((), ())),
        precision=lax.Precision.HIGHEST,
        preferred_element_type=jnp.float32,
    )
    preconditioned = lax.psum(kernel_part, "wide")
    rows = queries // n_narrow
    root = jnp.sqrt(jnp.float32(width))
    product = lax.dot_general(
        preconditioned,
        sketches,
        (((1,), (1,)), ((), ())),
        precision=lax.Precision.HIGHEST,
        preferred_element_type=jnp.float32,
    )
    scores = lax.psum_scatter(product / root, "narrow", scatter_dimension=0, tiled=True)
    total = lax.psum(local_squares, ("wide", "narrow"))
    late_scale = 1.0 / jnp.sqrt(total + epsilon)
    mine = lax.dynamic_slice_in_dim(late_scale, lax.axis_index("narrow") * rows, rows)
    scores = scores * mine[:, None]
    return scores


def split(value):
    high = value.astype(jnp.bfloat16)
    low = (value - high.astype(jnp.float32)).astype(jnp.bfloat16)
    return high, low


def fold(value):
    return (value & modulus) + (value >> 13)


def cos_sin(phase):
    centred = jnp.where(phase > modulus // 2, phase - modulus, phase)
    half = centred.astype(jnp.float32) * jnp.float32(math.pi / modulus)
    square = half * half
    sine = jnp.full_like(square, -1.0 / math.factorial(11))
    for power in (9, 7, 5, 3, 1):
        sine = sine * square + jnp.float32((-1.0) ** (power // 2) / math.factorial(power))
    sine = sine * half
    cosine = jnp.full_like(square, 1.0 / math.factorial(12))
    for power in (10, 8, 6, 4, 2, 0):
        cosine = cosine * square + jnp.float32((-1.0) ** (power // 2) / math.factorial(power))
    return 1.0 - 2.0 * sine * sine, 2.0 * sine * cosine


def kernel(
    n_wide, n_narrow, grads_ref, offsets_ref, seeds_ref, inv_hbm, sketch_hbm, out_ref,
    inv_f32, sketch_f32, inv_hi, inv_lo, sketch_hi, sketch_lo,
    part, from_core, to_x, from_x, mine, from_wide, owned,
    product, from_wide2, full, scored, from_narrow,
    sq_mine, sq_narrow, sq_sum, sq_wide,
    local_sem, core_send, core_recv, x_send, x_recv, wide_send, wide_recv,
    gather_send, gather_recv, wide2_send, wide2_recv, full_send, full_recv,
    last_send, last_recv, sqn_send, sqn_recv, sqw_send, sqw_recv,
):
    w = lax.axis_index("wide")
    n = lax.axis_index("narrow")
    sibling = n + 1 - 2 * lax.rem(n, 2)
    across = lax.rem(n + 2, n_narrow)
    diagonal = lax.rem(sibling + 2, n_narrow)
    width = seeds_ref.shape[1]
    block = width // n_wide
    rows = offsets_ref.shape[0]
    cols = grads_ref.shape[1] // 2
    queries = grads_ref.shape[0] // rows

    def wide_peer(s):
        return lax.rem(w + s, n_wide)

    def narrow_peer(s):
        return lax.rem(n + s, n_narrow)

    def remote(src, dst, send, recv, to_wide, to_narrow):
        return pltpu.make_async_remote_copy(
            src_ref=src, dst_ref=dst, send_sem=send, recv_sem=recv,
            device_id=(to_wide, to_narrow), device_id_type=pl.DeviceIdType.MESH,
        )

    load_inv = pltpu.make_async_copy(inv_hbm, inv_f32, local_sem.at[0])
    load_sketch = pltpu.make_async_copy(sketch_hbm, sketch_f32, local_sem.at[1])
    load_inv.start()
    load_sketch.start()

    barrier = pltpu.get_barrier_semaphore()
    for s in range(1, n_wide):
        pl.semaphore_signal(barrier, inc=1, device_id=(wide_peer(s), n), device_id_type=pl.DeviceIdType.MESH)
    for s in range(1, n_narrow):
        pl.semaphore_signal(barrier, inc=1, device_id=(w, narrow_peer(s)), device_id_type=pl.DeviceIdType.MESH)

    grads = grads_ref[...]
    squares = jnp.square(grads[:, :cols].astype(jnp.float32))
    by_query = squares[:queries]
    for r in range(1, rows):
        by_query = by_query + squares[r * queries : (r + 1) * queries]
    by_query = jnp.broadcast_to(jnp.sum(by_query, axis=1, keepdims=True), (queries, 128))
    mine_rows = queries // n_narrow
    group = lax.broadcasted_iota(jnp.int32, (mine_rows, 128), 1) // (128 // n_narrow)
    tile = by_query[:mine_rows]
    for j in range(1, n_narrow):
        tile = jnp.where(group == j, by_query[j * mine_rows : (j + 1) * mine_rows], tile)
    sq_mine[...] = tile

    bases = [fold(offsets_ref[r] + w * cols) for r in range(rows)]
    steps = cols // 16

    def project(slab):
        def chunk(j, carry):
            units = []
            for half in range(2):
                start = pl.multiple_of((2 * j + half) * block + slab * 128, 128)
                units.append(seeds_ref[:, pl.ds(start, 128)])
            seeds = jnp.concatenate(units, axis=1)
            mult = fold(seeds[0:1])
            add = seeds[1:2]
            at = lax.broadcasted_iota(jnp.int32, (steps + 16, 256), 0)
            factor = jnp.where(at < steps, at * 16, at - steps)
            col_cos, col_sin = cos_sin(fold(fold(factor * mult)))
            at = lax.broadcasted_iota(jnp.int32, (8, 256), 0)
            base = jnp.full((8, 256), bases[0], jnp.int32)
            for r in range(1, rows):
                base = jnp.where(at == r, bases[r], base)
            row_cos, row_sin = cos_sin(fold(fold(base * mult + add)))
            low_cos, low_sin = col_cos[steps:], col_sin[steps:]
            cos_parts, sin_parts = [], []
            for h in range(steps):
                high_cos, high_sin = col_cos[h : h + 1], col_sin[h : h + 1]
                cos_parts.append(split(high_cos * low_cos - high_sin * low_sin))
                sin_parts.append(split(high_sin * low_cos + high_cos * low_sin))
            cos_table = jnp.concatenate([p[0] for p in cos_parts] + [p[1] for p in cos_parts], axis=0)
            sin_table = jnp.concatenate([p[0] for p in sin_parts] + [p[1] for p in sin_parts], axis=0)
            by_cos = jnp.dot(grads_ref[...], cos_table, preferred_element_type=jnp.float32)
            by_sin = jnp.dot(grads_ref[...], sin_table, preferred_element_type=jnp.float32)
            total = jnp.zeros((queries, 256), jnp.float32)
            for r in range(rows):
                here = slice(r * queries, (r + 1) * queries)
                total = total + (row_cos[r : r + 1] * by_cos[here] - row_sin[r : r + 1] * by_sin[here])
            part[slab, 2 * j] = total[:, :128]
            part[slab, 2 * j + 1] = total[:, 128:]
            return carry

        lax.fori_loop(0, n_wide // 2, chunk, 0)

    project(diagonal)
    pl.semaphore_wait(barrier, n_wide + n_narrow - 2)
    core_copies = []
    copy = remote(part.at[diagonal], from_core.at[0], core_send.at[0], core_recv.at[0], w, sibling)
    copy.start()
    core_copies.append(copy)
    sqn_copies = []
    for s in range(1, n_narrow):
        copy = remote(sq_mine, sq_narrow.at[s - 1], sqn_send.at[s - 1], sqn_recv.at[s - 1], w, narrow_peer(s))
        copy.start()
        sqn_copies.append(copy)
    project(sibling)
    copy = remote(part.at[sibling], from_core.at[1], core_send.at[1], core_recv.at[1], w, sibling)
    copy.start()
    core_copies.append(copy)
    project(across)
    core_copies[0].wait_recv()
    order = [*range(1, n_wide), 0]
    x_copies = []
    for s in order:
        at = wide_peer(s)
        to_x[at] = part[across, at] + from_core[0, at]
        copy = remote(to_x.at[at], from_x.at[at], x_send.at[s], x_recv.at[s], w, across)
        copy.start()
        x_copies.append(copy)
    project(n)
    core_copies[1].wait_recv()
    wide_copies = []
    for s, x_copy in zip(order, x_copies):
        at = wide_peer(s)
        x_copy.wait_recv()
        mine[at] = part[n, at] + from_core[1, at] + from_x[at]
        if s:
            copy = remote(mine.at[at], from_wide.at[s - 1], wide_send.at[s - 1], wide_recv.at[s - 1], at, n)
            copy.start()
            wide_copies.append(copy)
    for copy in sqn_copies:
        copy.wait_recv()
    total = sq_mine[...]
    for s in range(1, n_narrow):
        total = total + sq_narrow[s - 1]
    sq_sum[...] = total
    sqw_copies = []
    for s in range(1, n_wide):
        copy = remote(sq_sum, sq_wide.at[s - 1], sqw_send.at[s - 1], sqw_recv.at[s - 1], wide_peer(s), n)
        copy.start()
        sqw_copies.append(copy)
    load_inv.wait()
    load_sketch.wait()
    slab_rows = 32

    def split_inv(i, carry):
        at = pl.ds(pl.multiple_of(i * slab_rows, slab_rows), slab_rows)
        inv_hi[at, :], inv_lo[at, :] = split(inv_f32[at, :])
        return carry

    def split_sketch(i, carry):
        at = pl.ds(pl.multiple_of(i * slab_rows, slab_rows), slab_rows)
        sketch_hi[at, :], sketch_lo[at, :] = split(sketch_f32[at, :])
        return carry

    lax.fori_loop(0, inv_f32.shape[0] // slab_rows, split_inv, 0)
    lax.fori_loop(0, sketch_f32.shape[0] // slab_rows, split_sketch, 0)

    total = mine[w]
    for s in range(1, n_wide):
        wide_copies[s - 1].wait_recv()
        total = total + from_wide[s - 1]
    owned[n] = total
    gather_copies = []
    for s in range(1, n_narrow):
        copy = remote(owned.at[n], owned.at[n], gather_send.at[s - 1], gather_recv.at[s - 1], w, narrow_peer(s))
        copy.start()
        gather_copies.append(copy)
    for copy in gather_copies:
        copy.wait_recv()
    high, low = split(jnp.concatenate([owned[i] for i in range(n_narrow)], axis=1))
    both = jnp.dot(jnp.concatenate([high, low], axis=0), inv_hi[...], preferred_element_type=jnp.float32)
    both = both[:queries] + both[queries:] + jnp.dot(high, inv_lo[...], preferred_element_type=jnp.float32)
    for i in range(n_wide):
        product[i] = both[:, i * 128 : (i + 1) * 128]
    wide2_copies = []
    for s in range(1, n_wide):
        at = wide_peer(s)
        copy = remote(product.at[at], from_wide2.at[s - 1], wide2_send.at[s - 1], wide2_recv.at[s - 1], at, n)
        copy.start()
        wide2_copies.append(copy)
    total = sq_sum[...]
    for s in range(1, n_wide):
        sqw_copies[s - 1].wait_recv()
        total = total + sq_wide[s - 1]
    own_squares = jnp.max(jnp.where(group == n, total, 0.0), axis=1, keepdims=True)
    scale = 1.0 / jnp.sqrt(own_squares + epsilon)
    scale = scale * jnp.float32(1.0 / math.sqrt(width))

    total = product[w]
    for s in range(1, n_wide):
        wide2_copies[s - 1].wait_recv()
        total = total + from_wide2[s - 1]
    full[w] = total
    full_copies = []
    for s in range(1, n_wide):
        copy = remote(full.at[w], full.at[w], full_send.at[s - 1], full_recv.at[s - 1], wide_peer(s), n)
        copy.start()
        full_copies.append(copy)
    for copy in full_copies:
        copy.wait_recv()
    high, low = split(jnp.concatenate([full[i] for i in range(n_wide)], axis=1))
    last = (((1,), (1,)), ((), ()))
    both = lax.dot_general(jnp.concatenate([high, low], axis=0), sketch_hi[...], last, preferred_element_type=jnp.float32)
    both = both[:queries] + both[queries:] + lax.dot_general(
        high, sketch_lo[...], last, preferred_element_type=jnp.float32
    )
    for i in range(n_narrow):
        scored[i] = both[i * mine_rows : (i + 1) * mine_rows]
    last_copies = []
    for s in range(1, n_narrow):
        at = narrow_peer(s)
        copy = remote(scored.at[at], from_narrow.at[s - 1], last_send.at[s - 1], last_recv.at[s - 1], w, at)
        copy.start()
        last_copies.append(copy)
    total = scored[n]
    for s in range(1, n_narrow):
        last_copies[s - 1].wait_recv()
        total = total + from_narrow[s - 1]
    out_ref[...] = total * scale
    for group_copies in (
        core_copies, x_copies, wide_copies, sqn_copies, sqw_copies, gather_copies, wide2_copies, full_copies, last_copies,
    ):
        for copy in group_copies:
            copy.wait_send()


def fused(n_wide, n_narrow, gradients, offsets, seeds, inv_kernel, sketches):
    queries, rows, cols = gradients.shape
    width = seeds.shape[1]
    depth, span = inv_kernel.shape
    trains = sketches.shape[0]
    grads = gradients.transpose(1, 0, 2).reshape(rows * queries, cols)
    grads = jnp.concatenate([grads, grads], axis=1)
    unit = (queries, 128)
    mine_rows = queries // n_narrow
    f32, bf16 = jnp.float32, jnp.bfloat16

    def sems(count):
        return [pltpu.SemaphoreType.DMA((count,))] * 2

    vmem = pl.BlockSpec(memory_space=pltpu.VMEM)
    return pl.pallas_call(
        functools.partial(kernel, n_wide, n_narrow),
        out_shape=jax.ShapeDtypeStruct((mine_rows, trains), f32),
        in_specs=[
            vmem,
            pl.BlockSpec(memory_space=pltpu.SMEM),
            vmem,
            pl.BlockSpec(memory_space=pl.ANY),
            pl.BlockSpec(memory_space=pl.ANY),
        ],
        out_specs=vmem,
        scratch_shapes=[
            pltpu.VMEM((depth, span), f32),
            pltpu.VMEM((trains, span), f32),
            pltpu.VMEM((depth, span), bf16),
            pltpu.VMEM((depth, span), bf16),
            pltpu.VMEM((trains, span), bf16),
            pltpu.VMEM((trains, span), bf16),
            pltpu.VMEM((n_narrow, n_wide) + unit, f32),
            pltpu.VMEM((2, n_wide) + unit, f32),
            pltpu.VMEM((n_wide,) + unit, f32),
            pltpu.VMEM((n_wide,) + unit, f32),
            pltpu.VMEM((n_wide,) + unit, f32),
            pltpu.VMEM((n_wide - 1,) + unit, f32),
            pltpu.VMEM((n_narrow,) + unit, f32),
            pltpu.VMEM((n_wide,) + unit, f32),
            pltpu.VMEM((n_wide - 1,) + unit, f32),
            pltpu.VMEM((n_wide,) + unit, f32),
            pltpu.VMEM((n_narrow, mine_rows, trains), f32),
            pltpu.VMEM((n_narrow - 1, mine_rows, trains), f32),
            pltpu.VMEM((mine_rows, 128), f32),
            pltpu.VMEM((n_narrow - 1, mine_rows, 128), f32),
            pltpu.VMEM((mine_rows, 128), f32),
            pltpu.VMEM((n_wide - 1, mine_rows, 128), f32),
            pltpu.SemaphoreType.DMA((2,)),
            *sems(2),
            *sems(n_wide),
            *sems(n_wide - 1),
            *sems(n_narrow - 1),
            *sems(n_wide - 1),
            *sems(n_wide - 1),
            *sems(n_narrow - 1),
            *sems(n_narrow - 1),
            *sems(n_wide - 1),
        ],
        compiler_params=pltpu.CompilerParams(
            collective_id=0, has_side_effects=True, vmem_limit_bytes=32 * 1024 * 1024
        ),
    )(grads, offsets, seeds, inv_kernel, sketches)


def solution(mesh):
    placed = (P(None, "narrow", "wide"), P("narrow"), P(), P("wide", "narrow"), P("wide", "narrow"))
    n_wide, n_narrow = mesh.shape["wide"], mesh.shape["narrow"]

    def local(gradients, offsets, seeds, inv_kernel, sketches):
        queries, rows, cols = gradients.shape
        fits = (
            seeds.shape[1] == n_wide * n_narrow * 128
            and n_narrow == 4
            and n_wide % 2 == 0
            and cols == 128
            and rows <= 8
            and queries % (8 * n_narrow) == 0
            and sketches.shape[0] == 128
        )
        if fits:
            return fused(n_wide, n_narrow, gradients, offsets, seeds, inv_kernel, sketches)
        return body(gradients, offsets, seeds, inv_kernel, sketches)

    return jax.shard_map(
        local, mesh=mesh, in_specs=placed, out_specs=P("narrow", "wide"), check_vma=False
    )
```

profile of v0, /device:TPU:0, one launch (start us, length us, event | category | flops | bytes accessed | tf_op | source)
XLA Modules:
  0.0 38.8 jit_solution(4973921600461730848)
XLA Ops:
  0.0 0.8 %copy.6 = bf16[4,32,128]{2,1,0:T(8,128)(2,1)S(1)} copy(bf16[4,32,128]{2,0,1:T(4,128)(2,1)} %bitcast.3) | data formatting | bytes 65536 | tf_op jit(solution)/shard_map/transpose | solution.py:334
  0.8 0.0 copy-start
  0.8 1.6 %copy-done = f32[512,1024]{1,0:T(8,128)S(1)} copy-done((f32[512,1024]{1,0:T(8,128)S(1)}, f32[512,1024]{1,0:T(8,128)}, u32[]{:S(2)}) %copy-start) | copy-done | bytes 2097176
  2.4 0.0 copy-start.1
  2.4 1.0 %copy-done.1 = f32[128,1024]{1,0:T(8,128)S(1)} copy-done((f32[128,1024]{1,0:T(8,128)S(1)}, f32[128,1024]{1,0:T(8,128)}, u32[]{:S(2)}) %copy-start.1) | copy-done | bytes 524312
  3.4 0.0 copy-start.2
  3.4 0.8 %copy-done.2 = s32[2,4096]{1,0:T(2,128)S(1)} copy-done((s32[2,4096]{1,0:T(2,128)S(1)}, s32[2,4096]{1,0:T(2,128)}, u32[]{:S(2)}) %copy-start.2) | copy-done | bytes 32792
  4.2 0.0 copy-start.3
  4.2 0.7 %copy-done.3 = s32[4]{0:T(128)S(1)} copy-done((s32[4]{0:T(128)S(1)}, s32[4]{0:T(128)}, u32[]{:S(2)}) %copy-start.3) | copy-done | bytes 40
  4.8 33.4 %shard_map.55 = f32[8,128]{1,0:T(8,128)S(1)} custom-call(bf16[128,256]{1,0:T(8,128)(2,1)S(1)} %pad_maximum_fusion.grads_ref, s32[4]{0:T(128)S(1)} %copy-done.3, s32[2,4096]{1,0:T(2,128)S(1)} %copy-done.2, f32[512,1024]{1,0:T(8,128)S(1)} %copy-done, f32[128,1024]{1,0:T(8,128)S(1)} %copy-done.1), custom_call_target="tpu_custom_call" | custom-call | tf_op jit(solution)/shard_map/pallas_call | solution.py:344
  38.2 0.6 %copy.8 = f32[8,128]{1,0:T(8,128)} copy(f32[8,128]{1,0:T(8,128)S(1)} %shard_map.55) | data formatting | bytes 8192
  (1 shorter events, 0.0 us)
Async XLA Ops:
  0.8 1.6 %copy-start = (f32[512,1024]{1,0:T(8,128)S(1)}, f32[512,1024]{1,0:T(8,128)}, u32[]{:S(2)}) copy-start(f32[512,1024]{1,0:T(8,128)} %inv_hbm.1) | copy-start | bytes 6291460
  2.4 1.0 %copy-start.1 = (f32[128,1024]{1,0:T(8,128)S(1)}, f32[128,1024]{1,0:T(8,128)}, u32[]{:S(2)}) copy-start(f32[128,1024]{1,0:T(8,128)} %sketch_hbm.1) | copy-start | bytes 1572868
  3.4 0.8 %copy-start.2 = (s32[2,4096]{1,0:T(2,128)S(1)}, s32[2,4096]{1,0:T(2,128)}, u32[]{:S(2)}) copy-start(s32[2,4096]{1,0:T(2,128)} %seeds_ref.1) | copy-start | bytes 98308
  4.2 0.7 %copy-start.3 = (s32[4]{0:T(128)S(1)}, s32[4]{0:T(128)}, u32[]{:S(2)}) copy-start(s32[4]{0:T(128)} %offsets_ref.1) | copy-start | bytes 52
where the time goes:
time: 39.2 us; the launch traced here: 38.8 us
  Pallas kernels  33.4 us (85%)
  local copies, waits for them, and re-layouts  5.4 us (14%)
    pallas_call x1, Pallas kernels, fused(): pl.pallas_call(functools.partial(kernel, n_wide, n_narrow), out_shape=jax...  33.4 us
    unnamed x9, local copies, waits for them, and re-layouts  4.63 us

commit v1 on v0

--- a/solution.py
+++ b/solution.py
@@ -97,8 +97,8 @@
 
 
 def kernel(
-    n_wide, n_narrow, grads_ref, offsets_ref, seeds_ref, inv_hbm, sketch_hbm, out_ref,
-    inv_f32, sketch_f32, inv_hi, inv_lo, sketch_hi, sketch_lo,
+    n_wide, n_narrow, grads_hbm, offsets_hbm, seeds_hbm, inv_hbm, sketch_hbm, out_ref,
+    grads_in, grads_f32, grads_ref, offsets_ref, seeds_ref, inv_f32, sketch_f32, inv_hi, inv_lo, sketch_hi, sketch_lo,
     part, from_core, to_x, from_x, mine, from_wide, owned,
     product, from_wide2, full, scored, from_narrow,
     sq_mine, sq_narrow, sq_sum, sq_wide,
@@ -114,8 +114,7 @@
     width = seeds_ref.shape[1]
     block = width // n_wide
     rows = offsets_ref.shape[0]
-    cols = grads_ref.shape[1] // 2
-    queries = grads_ref.shape[0] // rows
+    queries, _, cols = grads_in.shape
 
     def wide_peer(s):
         return lax.rem(w + s, n_wide)
@@ -131,6 +130,12 @@
 
     load_inv = pltpu.make_async_copy(inv_hbm, inv_f32, local_sem.at[0])
     load_sketch = pltpu.make_async_copy(sketch_hbm, sketch_f32, local_sem.at[1])
+    load_grads = pltpu.make_async_copy(grads_hbm, grads_in, local_sem.at[2])
+    load_seeds = pltpu.make_async_copy(seeds_hbm, seeds_ref, local_sem.at[3])
+    load_offsets = pltpu.make_async_copy(offsets_hbm, offsets_ref, local_sem.at[4])
+    load_grads.start()
+    load_seeds.start()
+    load_offsets.start()
     load_inv.start()
     load_sketch.start()
 
@@ -140,11 +145,15 @@
     for s in range(1, n_narrow):
         pl.semaphore_signal(barrier, inc=1, device_id=(w, narrow_peer(s)), device_id_type=pl.DeviceIdType.MESH)
 
-    grads = grads_ref[...]
-    squares = jnp.square(grads[:, :cols].astype(jnp.float32))
-    by_query = squares[:queries]
-    for r in range(1, rows):
-        by_query = by_query + squares[r * queries : (r + 1) * queries]
+    load_grads.wait()
+    grads_f32[...] = grads_in[...].astype(jnp.float32)
+    by_query = jnp.zeros((queries, cols), jnp.float32)
+    for r in range(rows):
+        one_row = grads_f32[:, r, :]
+        by_query = by_query + jnp.square(one_row)
+        one_row = one_row.astype(jnp.bfloat16)
+        grads_ref[r * queries : (r + 1) * queries, :cols] = one_row
+        grads_ref[r * queries : (r + 1) * queries, cols:] = one_row
     by_query = jnp.broadcast_to(jnp.sum(by_query, axis=1, keepdims=True), (queries, 128))
     mine_rows = queries // n_narrow
     group = lax.broadcasted_iota(jnp.int32, (mine_rows, 128), 1) // (128 // n_narrow)
@@ -153,6 +162,8 @@
         tile = jnp.where(group == j, by_query[j * mine_rows : (j + 1) * mine_rows], tile)
     sq_mine[...] = tile
 
+    load_offsets.wait()
+    load_seeds.wait()
     bases = [fold(offsets_ref[r] + w * cols) for r in range(rows)]
     steps = cols // 16
 
@@ -331,8 +342,6 @@
     width = seeds.shape[1]
     depth, span = inv_kernel.shape
     trains = sketches.shape[0]
-    grads = gradients.transpose(1, 0, 2).reshape(rows * queries, cols)
-    grads = jnp.concatenate([grads, grads], axis=1)
     unit = (queries, 128)
     mine_rows = queries // n_narrow
     f32, bf16 = jnp.float32, jnp.bfloat16
@@ -340,19 +349,17 @@
     def sems(count):
         return [pltpu.SemaphoreType.DMA((count,))] * 2
 
-    vmem = pl.BlockSpec(memory_space=pltpu.VMEM)
     return pl.pallas_call(
         functools.partial(kernel, n_wide, n_narrow),
         out_shape=jax.ShapeDtypeStruct((mine_rows, trains), f32),
-        in_specs=[
-            vmem,
-            pl.BlockSpec(memory_space=pltpu.SMEM),
-            vmem,
-            pl.BlockSpec(memory_space=pl.ANY),
-            pl.BlockSpec(memory_space=pl.ANY),
-        ],
-        out_specs=vmem,
+        in_specs=[pl.BlockSpec(memory_space=pltpu.HBM)] * 5,
+        out_specs=pl.BlockSpec(memory_space=pltpu.VMEM),
         scratch_shapes=[
+            pltpu.VMEM((queries, rows, cols), bf16),
+            pltpu.VMEM((queries, rows, cols), f32),
+            pltpu.VMEM((rows * queries, 2 * cols), bf16),
+            pltpu.SMEM((rows,), jnp.int32),
+            pltpu.VMEM((2, width), jnp.int32),
             pltpu.VMEM((depth, span), f32),
             pltpu.VMEM((trains, span), f32),
             pltpu.VMEM((depth, span), bf16),
@@ -375,7 +382,7 @@
             pltpu.VMEM((n_narrow - 1, mine_rows, 128), f32),
             pltpu.VMEM((mine_rows, 128), f32),
             pltpu.VMEM((n_wide - 1, mine_rows, 128), f32),
-            pltpu.SemaphoreType.DMA((2,)),
+            pltpu.SemaphoreType.DMA((5,)),
             *sems(2),
             *sems(n_wide),
             *sems(n_wide - 1),
@@ -387,9 +394,9 @@
             *sems(n_wide - 1),
         ],
         compiler_params=pltpu.CompilerParams(
-            collective_id=0, has_side_effects=True, vmem_limit_bytes=32 * 1024 * 1024
+            collective_id=0, has_side_effects=True, vmem_limit_bytes=63 * 1024 * 1024
         ),
-    )(grads, offsets, seeds, inv_kernel, sketches)
+    )(gradients, offsets, seeds, inv_kernel, sketches)
 
 
 def solution(mesh):

time: 39.2 us -> 34.7 us (0.89)
  local copies, waits for them, and re-layouts: 5.4 us -> 1.28 us
    unnamed x9 -> x1, local copies, waits for them, and re-layouts: 4.63 us -> 1.28 us
    transpose x1 -> x0, local copies, waits for them, and re-layouts: 0.76 us -> none  [fused(): grads = gradients.transpose(1, 0, 2).reshape(rows * queries, cols)]
where the time goes in v1:
time: 34.7 us; the launch traced here: 34.6 us
  Pallas kernels  33.3 us (96%)
  local copies, waits for them, and re-layouts  1.28 us (4%)
    pallas_call x1, Pallas kernels, fused(): pl.pallas_call(functools.partial(kernel, n_wide, n_narrow), out_shape=jax...  33.3 us
    unnamed x1, local copies, waits for them, and re-layouts  1.28 us

profile of v1, /device:TPU:0, one launch (start us, length us, event | category | flops | bytes accessed | tf_op | source)
XLA Modules:
  0.0 34.6 jit_solution(9435078447569106387)
XLA Ops:
  0.0 33.3 %shard_map.55 = f32[8,128]{1,0:T(8,128)} custom-call(bf16[32,4,128]{2,1,0:T(4,128)(2,1)} %grads_hbm.1, s32[4]{0:T(128)} %offsets_hbm.1, s32[2,4096]{1,0:T(2,128)} %seeds_hbm.1, f32[512,1024]{1,0:T(8,128)} %inv_hbm.1, f32[128,1024]{1,0:T(8,128)} %sketch_hbm.1), custom_call_target="tpu_custom_call" | custom-call | tf_op jit(solution)/shard_map/pallas_call | solution.py:352
  33.3 1.3 %copy.7 = f32[8,128]{1,0:T(8,128)} copy(f32[8,128]{1,0:T(8,128)} %shard_map.55) | data formatting | bytes 8192

commit v2 on v1

--- a/solution.py
+++ b/solution.py
@@ -215,10 +215,6 @@
         copy = remote(sq_mine, sq_narrow.at[s - 1], sqn_send.at[s - 1], sqn_recv.at[s - 1], w, narrow_peer(s))
         copy.start()
         sqn_copies.append(copy)
-    project(sibling)
-    copy = remote(part.at[sibling], from_core.at[1], core_send.at[1], core_recv.at[1], w, sibling)
-    copy.start()
-    core_copies.append(copy)
     project(across)
     core_copies[0].wait_recv()
     order = [*range(1, n_wide), 0]
@@ -229,6 +225,10 @@
         copy = remote(to_x.at[at], from_x.at[at], x_send.at[s], x_recv.at[s], w, across)
         copy.start()
         x_copies.append(copy)
+    project(sibling)
+    copy = remote(part.at[sibling], from_core.at[1], core_send.at[1], core_recv.at[1], w, sibling)
+    copy.start()
+    core_copies.append(copy)
     project(n)
     core_copies[1].wait_recv()
     wide_copies = []

time: 34.7 us -> 34.2 us (0.986)
  Pallas kernels: 33.3 us -> 32.7 us
    pallas_call x1, Pallas kernels: 33.3 us -> 32.7 us  [fused(): pl.pallas_call(functools.partial(kernel, n_wide, n_narrow), out_shape=jax...]
where the time goes in v2:
time: 34.2 us; the launch traced here: 34 us
  Pallas kernels  32.7 us (96%)
  local copies, waits for them, and re-layouts  1.28 us (4%)
    pallas_call x1, Pallas kernels, fused(): pl.pallas_call(functools.partial(kernel, n_wide, n_narrow), out_shape=jax...  32.7 us
    unnamed x1, local copies, waits for them, and re-layouts  1.28 us

profile of v2, /device:TPU:0, one launch (start us, length us, event | category | flops | bytes accessed | tf_op | source)
XLA Modules:
  0.0 34.0 jit_solution(17221551176154247444)
XLA Ops:
  0.0 32.7 %shard_map.55 = f32[8,128]{1,0:T(8,128)} custom-call(bf16[32,4,128]{2,1,0:T(4,128)(2,1)} %grads_hbm.1, s32[4]{0:T(128)} %offsets_hbm.1, s32[2,4096]{1,0:T(2,128)} %seeds_hbm.1, f32[512,1024]{1,0:T(8,128)} %inv_hbm.1, f32[128,1024]{1,0:T(8,128)} %sketch_hbm.1), custom_call_target="tpu_custom_call" | custom-call | tf_op jit(solution)/shard_map/pallas_call | solution.py:352
  32.7 1.3 %copy.7 = f32[8,128]{1,0:T(8,128)} copy(f32[8,128]{1,0:T(8,128)} %shard_map.55) | data formatting | bytes 8192
